TPU v7x, 256 devices: a whole 4x4x8 slice. The times are simulated.
256 devices in a mesh: ping: 4 (over z_lo), band: 64 (over y, z_hi, x, core).
Axes of the slice: x: 4, y: 4, z: 8 (z_hi: 2, z_lo: 4; z = z_hi * 4 + z_lo), core: 2. Of those that a mesh axis runs over, the one named last changes fastest.
Arguments:
- staves: bfloat16 [2, 64, 256, 8, 512], P(None, 'ping', 'band'), may hold values from -6 to 6
- weights: bfloat16 [2, 256, 512, 512], P(None, 'band'), may hold values from -0.25 to 0.25
- replica: float32 [2, 2048], replicated, may hold values from -5 to 5
- start: int32 [64, 512], P('ping', 'band'), may hold values from 0 to 1535
- length: int32 [64, 512], P('ping', 'band'), may hold values from 64 to 512
Outputs:
- centroid: float32 [64, 512], P('ping', 'band')
- energy: float32 [64, 512], P('ping', 'band')
Inputs may be any that keep to these rules, and one draw needn't show every extreme that they name: Every window lies inside the beam's samples: start + length <= 2048.
All inputs are finite; a program needn't handle non-finite values.
Results may differ from a plain program's by a relative error of at most 0.0004.
Values may be sent and summed in bfloat16 or wider, within the bound.
A program may use at most 128 MiB of HBM per device.

v0:
```python
import math

import jax
import jax.numpy as jnp
from jax import lax
from jax.sharding import PartitionSpec as P

TAPS = (1.0, 2.0, 3.0, 4.0, 5.0, 4.0, 3.0, 2.0, 1.0)


def extended(array, sides, width):
    for axis, dim in sides:
        count, length = (lax.axis_size(axis), array.shape[dim])
        up = [(i, (i + 1) % count) for i in range(count - 1)]
        down = [(j, i) for i, j in up]
        last = lax.slice_in_dim(array, length - width, length, axis=dim)
        initial = lax.slice_in_dim(array, 0, width, axis=dim)
        before = lax.ppermute(last, axis, up)
        after = lax.ppermute(initial, axis, down)
        array = jnp.concatenate([before, array, after], axis=dim)
    return array


def dft_tables(length_total):
    freqs = jnp.arange(length_total, dtype=jnp.int32)
    phases = freqs[:, None] * freqs[None, :] % length_total
    angles = phases.astype(jnp.float32) * (2.0 * math.pi / length_total)
    return (jnp.cos(angles).astype(jnp.bfloat16), jnp.sin(angles).astype(jnp.bfloat16))


def envelope_rows(spec_re, spec_im, replica, cos_table, sin_table):
    comp_re = (spec_re * replica[0] + spec_im * replica[1]).astype(jnp.bfloat16)
    comp_im = (spec_im * replica[0] - spec_re * replica[1]).astype(jnp.bfloat16)
    wave_re = jnp.dot(comp_re, cos_table, preferred_element_type=jnp.float32) - jnp.dot(
        comp_im, sin_table, preferred_element_type=jnp.float32
    )
    wave_im = jnp.dot(comp_re, sin_table, preferred_element_type=jnp.float32) + jnp.dot(
        comp_im, cos_table, preferred_element_type=jnp.float32
    )
    return (wave_re * wave_re + wave_im * wave_im) * (1.0 / (16.0 * cos_table.shape[0]))


def smooth_pings(padded, first_ping, total_pings, ping_count):
    positions = first_ping + jnp.arange(ping_count + 8, dtype=jnp.int32) - 4
    inside = ((positions >= 0) & (positions < total_pings)).astype(jnp.float32)
    summed = jnp.zeros((ping_count,) + padded.shape[1:], jnp.float32)
    weight_sum = jnp.zeros((ping_count,), jnp.float32)
    for offset in range(9):
        summed = summed + TAPS[offset] * padded[offset : offset + ping_count]
        weight_sum = weight_sum + TAPS[offset] * inside[offset : offset + ping_count]
    return summed / weight_sum[:, None, None]


def window_stats(smoothed, start, length):
    samples = jnp.arange(smoothed.shape[-1], dtype=jnp.int32)
    window_start = start[..., None]
    finish = (start + length)[..., None]
    inside = (samples >= window_start) & (samples < finish)
    offsets = samples.astype(jnp.float32) - start.astype(jnp.float32)[..., None] + 0.5
    energy_total = jnp.sum(jnp.where(inside, smoothed, 0.0), axis=-1)
    moment = jnp.sum(jnp.where(inside, smoothed * offsets, 0.0), axis=-1)
    widths = length.astype(jnp.float32)
    return (moment / (widths * (energy_total + 1e-06)), energy_total / widths)


def local(staves, weights, replica, start, length):
    ping_index = lax.axis_index("ping")
    ping_total = lax.axis_size("ping")
    beam_re = jnp.einsum(
        "pkfs,ksb->kpfb", staves[0], weights[0], preferred_element_type=jnp.float32
    ) - jnp.einsum("pkfs,ksb->kpfb", staves[1], weights[1], preferred_element_type=jnp.float32)
    beam_im = jnp.einsum(
        "pkfs,ksb->kpfb", staves[0], weights[1], preferred_element_type=jnp.float32
    ) + jnp.einsum("pkfs,ksb->kpfb", staves[1], weights[0], preferred_element_type=jnp.float32)
    beams = jnp.stack([beam_re, beam_im]).astype(jnp.bfloat16)
    cos_table, sin_table = dft_tables(replica.shape[1])
    turned = lax.all_to_all(beams, "band", split_axis=4, concat_axis=1, tiled=True)
    pings_here = turned.shape[2]
    beams_here = turned.shape[4]
    flat_rows = jnp.transpose(turned, (0, 2, 4, 1, 3)).reshape(2, pings_here * beams_here, -1)
    energy_rows = envelope_rows(
        flat_rows[0].astype(jnp.float32),
        flat_rows[1].astype(jnp.float32),
        replica,
        cos_table,
        sin_table,
    )
    envelope = energy_rows.reshape(pings_here, beams_here, -1)
    ping_count = envelope.shape[0]
    padded = extended(envelope.astype(jnp.bfloat16), (("ping", 0),), 4).astype(envelope.dtype)
    smoothed = smooth_pings(padded, ping_index * ping_count, ping_total * ping_count, ping_count)
    centroid, energy = window_stats(smoothed, start, length)
    return (centroid, energy)


def solution(mesh):
    in_specs = (
        P(None, "ping", "band", None, None),
        P(None, "band", None, None),
        P(),
        P("ping", "band"),
        P("ping", "band"),
    )
    out_specs = (P("ping", "band"), P("ping", "band"))
    return jax.shard_map(local, mesh=mesh, in_specs=in_specs, out_specs=out_specs, check_vma=False)
```

profile of v0, /device:TPU:1, one launch (start us, length us, event | category | flops | bytes accessed | tf_op | source)
XLA Modules:
  0.0 426.1 jit_solution(4095808901645931847)
XLA Ops:
  0.6 1.3 fusion.72
  1.9 2.1 fusion.19
  4.0 0.0 copy-start.1
  4.0 0.0 copy-start.2
  4.0 0.0 copy-start
  4.0 2.1 fusion.17
  6.1 2.1 fusion.41
  8.2 2.1 fusion.44
  10.2 0.1 pad_maximum_fusion
  10.3 12.1 %copy.51 = bf16[2,4,16,8,512]{2,3,1,0,4:T(8,128)(2,1)} copy(bf16[2,4,16,8,512]{4,3,2,1,0:T(8,128)(2,1)S(1)} %pad_maximum_fusion) | data formatting | bytes 2097152 | tf_op jit(solution)/shard_map/stack | solution.py:75
  22.4 12.5 %reshape.29 = bf16[64,2,4096]{2,1,0:T(2,128)(2,1)} reshape(bf16[512,2,4,8,16]{4,3,2,1,0:T(8,128)(2,1)} %bitcast.65) | data formatting | bytes 2097152
  34.9 15.9 %all-to-all-start = ((bf16[64,2,4096]{2,1,0:T(2,128)(2,1)}), bf16[64,2,4096]{2,1,0:T(2,128)(2,1)S(1)}, u32[]{:S(2)}, u32[]{:S(2)}) async-start(bf16[64,2,4096]{2,1,0:T(2,128)(2,1)} %reshape.29), calls=%async_computation | async-start | bytes 2097152 | tf_op jit(solution)/shard_map/all_to_all | solution.py:77
  50.8 0.0 copy-done.1
  50.8 0.0 copy-done.2
  50.9 0.0 copy-done
  50.9 27.5 %all-to-all-done = bf16[64,2,4096]{2,1,0:T(2,128)(2,1)S(1)} async-done(((bf16[64,2,4096]{2,1,0:T(2,128)(2,1)}), bf16[64,2,4096]{2,1,0:T(2,128)(2,1)S(1)}, u32[]{:S(2)}, u32[]{:S(2)}) %all-to-all-start) | async-done | bytes 1048608 | tf_op jit(solution)/shard_map/all_to_all | solution.py:77
  78.4 7.5 %reshape.30 = bf16[512,2,4,8,16]{4,3,2,1,0:T(8,128)(2,1)} reshape(bf16[64,2,4096]{2,1,0:T(2,128)(2,1)S(1)} %all-to-all-done) | data formatting | bytes 2097152
  85.9 16.3 %copy.53 = bf16[2,64,4,16,8,8]{3,5,4,2,1,0:T(8,128)(2,1)} copy(bf16[2,64,4,16,8,8]{3,4,2,0,5,1:T(8,128)(2,1)} %bitcast.66) | data formatting | bytes 2097152 | tf_op jit(solution)/shard_map/all_to_all | solution.py:77
  102.2 12.6 %copy.54 = bf16[2,256,16,8,8]{1,3,4,2,0:T(8,128)(2,1)S(1)} copy(bf16[2,256,16,8,8]{2,4,3,1,0:T(8,128)(2,1)} %bitcast.67) | data formatting | bytes 2097152 | tf_op jit(solution)/shard_map/all_to_all | solution.py:77
  114.8 0.3 slice_convert_fusion.1
  115.1 8.4 %copy.55 = f32[1,16,8,256,8]{4,3,2,1,0:T(8,128)} copy(f32[1,16,8,256,8]{3,4,2,1,0:T(8,128)S(1)} %get-tuple-element.12) | data formatting | bytes 2097152 | tf_op jit(solution)/shard_map/convert_element_type | solution.py:82
  123.5 12.6 %reshape.25 = f32[128,2048]{1,0:T(8,128)S(1)} reshape(f32[1,16,8,256,8]{4,3,2,1,0:T(8,128)} %copy.55) | data formatting | bytes 2097152 | tf_op jit(solution)/shard_map/convert_element_type | solution.py:82
  136.1 8.4 %copy.56 = f32[1,16,8,256,8]{4,3,2,1,0:T(8,128)} copy(f32[1,16,8,256,8]{3,4,2,1,0:T(8,128)S(1)} %get-tuple-element.13) | data formatting | bytes 2097152 | tf_op jit(solution)/shard_map/convert_element_type | solution.py:83
  144.6 12.6 %reshape.26 = f32[128,2048]{1,0:T(8,128)S(1)} reshape(f32[1,16,8,256,8]{4,3,2,1,0:T(8,128)} %copy.56) | data formatting | bytes 2097152 | tf_op jit(solution)/shard_map/convert_element_type | solution.py:83
  157.2 0.3 subtract_convert_fusion
  157.5 62.5 %fusion.7 = f32[128,2048]{1,0:T(8,128)S(1)} fusion(bf16[128,2048]{1,0:T(8,128)(2,1)S(1)} %get-tuple-element.11), kind=kOutput, calls=%fused_computation.12 | convolution fusion | flops 1136656384 | bytes 1572864 | tf_op jit(solution)/shard_map/dot_general | solution.py:34
  220.0 62.7 %fusion.6 = f32[128,2048]{1,0:T(8,128)S(1)} fusion(bf16[128,2048]{1,0:T(8,128)(2,1)S(1)} %get-tuple-element.10), kind=kOutput, calls=%fused_computation.11 | convolution fusion | flops 1136656384 | bytes 1572864 | tf_op jit(solution)/shard_map/dot_general | solution.py:37
  282.7 63.0 %fusion.11 = f32[128,2048]{1,0:T(8,128)S(1)} fusion(f32[128,2048]{1,0:T(8,128)S(1)} %fusion.7, bf16[128,2048]{1,0:T(8,128)(2,1)S(1)} %get-tuple-element.10), kind=kOutput, calls=%fused_computation.16 | convolution fusion | flops 1137180672 | bytes 2621440 | tf_op jit(solution)/shard_map/dot_general | solution.py:34
  345.7 63.0 %fusion.16 = bf16[128,2048]{1,0:T(8,128)(2,1)S(1)} fusion(f32[128,2048]{1,0:T(8,128)S(1)} %fusion.11, f32[128,2048]{1,0:T(8,128)S(1)} %fusion.6, bf16[128,2048]{1,0:T(8,128)(2,1)S(1)} %get-tuple-element.11), kind=kOutput, calls=%fused_computation.21 | convolution fusion | flops 1137967104 | bytes 3145728 | tf_op jit(solution)/shard_map/dot_general | solution.py:37
  408.8 8.0 %collective-permute-start = (bf16[4,8,2048]{2,1,0:T(8,128)(2,1)S(1)}, bf16[4,8,2048]{2,1,0:T(8,128)(2,1)S(1)}, u32[]{:S(2)}, u32[]{:S(2)}) collective-permute-start(bf16[4,8,2048]{2,1,0:T(8,128)(2,1)S(1)} %get-tuple-element.16), channel_id=1, source_target_pairs={{0,64},{64,128},{128,192},{1,65},{65,129},{129,193},{2,66},{66,130... | collective-permute-start | bytes 393224 | tf_op jit(solution)/shard_map/ppermute | solution.py:18
  416.8 1.3 collective-permute-start.1
  418.1 0.1 slice_add_fusion.1
  418.2 0.1 copy.47
  418.3 0.1 copy.58
  418.3 0.1 copy.48
  418.4 0.1 copy.57
  418.5 0.9 collective-permute-done
  419.4 3.8 collective-permute-done.1
  423.2 0.1 maximum_convert_fusion
  423.3 1.3 select_reduce_fusion
  424.6 0.7 copy.59
  425.2 0.7 copy.60
  (6 shorter events, 0.1 us)
Async XLA Ops:
  4.0 46.9 %copy-start.1 = (s32[16,8]{0,1:T(8,128)S(1)}, s32[16,8]{0,1:T(8,128)}, u32[]{:S(2)}) copy-start(s32[16,8]{0,1:T(8,128)} %param.8) | copy-start | bytes 1540
  4.0 46.9 %copy-start.2 = (s32[16,8]{0,1:T(8,128)S(1)}, s32[16,8]{0,1:T(8,128)}, u32[]{:S(2)}) copy-start(s32[16,8]{0,1:T(8,128)} %param.9) | copy-start | bytes 1540
  4.0 46.9 %copy-start = (f32[2,2048]{1,0:T(2,128)S(1)}, f32[2,2048]{1,0:T(2,128)}, u32[]{:S(2)}) copy-start(f32[2,2048]{1,0:T(2,128)} %param.7) | copy-start | bytes 49156
  34.9 43.5 %all-to-all-start = ((bf16[64,2,4096]{2,1,0:T(2,128)(2,1)}), bf16[64,2,4096]{2,1,0:T(2,128)(2,1)S(1)}, u32[]{:S(2)}, u32[]{:S(2)}) async-start(bf16[64,2,4096]{2,1,0:T(2,128)(2,1)} %reshape.29), calls=%async_computation | async-start | bytes 2097152 | tf_op jit(solution)/shard_map/all_to_all | solution.py:77
  408.8 10.6 %collective-permute-start = (bf16[4,8,2048]{2,1,0:T(8,128)(2,1)S(1)}, bf16[4,8,2048]{2,1,0:T(8,128)(2,1)S(1)}, u32[]{:S(2)}, u32[]{:S(2)}) collective-permute-start(bf16[4,8,2048]{2,1,0:T(8,128)(2,1)S(1)} %get-tuple-element.16), channel_id=1, source_target_pairs={{0,64},{64,128},{128,192},{1,65},{65,129},{129,193},{2,66},{66,130... | collective-permute-start | bytes 393224 | tf_op jit(solution)/shard_map/ppermute | solution.py:18
  416.8 6.3 %collective-permute-start.1 = (bf16[4,8,2048]{2,1,0:T(8,128)(2,1)S(1)}, bf16[4,8,2048]{2,1,0:T(8,128)(2,1)S(1)}, u32[]{:S(2)}, u32[]{:S(2)}) collective-permute-start(bf16[4,8,2048]{2,1,0:T(8,128)(2,1)S(1)} %get-tuple-element.17), channel_id=1, source_target_pairs={{64,0},{128,64},{192,128},{65,1},{129,65},{193,129},{66,2},{130,66... | collective-permute-start | bytes 393224 | tf_op jit(solution)/shard_map/ppermute | solution.py:19
where the time goes:
time: 431 us; the launch traced here: 426 us
  matrix products  259 us (60%)
  local copies, waits for them, and re-layouts  106 us (25%)
  waiting for transfers between devices  32.2 us (7%)
  starting transfers between devices  25.2 us (6%)
    dot_general x1, matrix products, envelope_rows(): jnp.dot(comp_re, sin_table, preferred_element_type=jnp.float32)  63 us
    dot_general x1, matrix products, envelope_rows(): jnp.dot(comp_im, sin_table, preferred_element_type=jnp.float32)  63 us
    dot_general x1, matrix products, envelope_rows(): jnp.dot(comp_im, cos_table, preferred_element_type=jnp.float32)  62.7 us
    dot_general x1, matrix products, envelope_rows(): jnp.dot(comp_re, cos_table, preferred_element_type=jnp.float32)  62.5 us
    all_to_all x2, local copies, waits for them, and re-layouts, local(): lax.all_to_all(beams, 'band', split_axis=4, concat_axis=1, tiled=True)  28.9 us
    all_to_all x1, waiting for transfers between devices, local(): lax.all_to_all(beams, 'band', split_axis=4, concat_axis=1, tiled=True)  27.5 us
    unnamed x12, local copies, waits for them, and re-layouts  21.5 us
    convert_element_type x2, local copies, waits for them, and re-layouts, local(): flat_rows[0].astype(jnp.float32)  21.1 us
  transfers between devices with their start and end apart: 3, of which 3 were waited for; matrix products, arithmetic and copies ran while one was open for 0% of the time, Pallas kernels for 0%

commit v1 on v0

v1 whole, which is shorter than its diff:
```python
import functools
import math

import ml_dtypes
import numpy as np

import jax
import jax.numpy as jnp
from jax import lax
from jax.experimental import pallas as pl
from jax.experimental.pallas import tpu as pltpu
from jax.sharding import PartitionSpec as P

MESH = pl.DeviceIdType.MESH
BINS, SPLIT, REACH = 8, 256, 4
TAPS = (1.0, 2.0, 3.0, 4.0, 5.0, 4.0, 3.0, 2.0, 1.0)


def tables(sources, bands_each):
    total = SPLIT * BINS
    turn = 2.0 * math.pi / total
    t1 = np.arange(SPLIT)
    band = (np.arange(sources)[None, :] * bands_each + np.arange(bands_each)[:, None]).reshape(-1)
    angle = ((t1[:, None] * band[None, :] * BINS) % total) * turn
    first = np.block([[np.cos(angle), -np.sin(angle)], [np.sin(angle), np.cos(angle)]])
    lane = np.arange(128)
    ping, small = lane // BINS, lane % BINS
    angle = ((t1[:, None] * small[None, :]) % total) * turn
    twiddle = np.stack([np.cos(angle), np.sin(angle)])
    same = ping[:, None] == ping[None, :]
    angle = ((small[:, None] * small[None, :]) % BINS) * (2.0 * math.pi / BINS)
    cos, sin = np.cos(angle) * same, np.sin(angle) * same
    second = np.block([[cos, sin], [-sin, cos]])
    above, below = ping + 16, ping - 16
    beside = np.where(ping < REACH, above, np.where(ping >= 16 - REACH, below, 1000))
    target = np.concatenate([ping, beside])
    kind = np.concatenate([small, small])
    smooth = np.maximum(5 - np.abs(ping[:, None] - target[None, :]), 0) * (small[:, None] == kind[None, :])
    half = ml_dtypes.bfloat16
    return first.astype(half), twiddle.astype(np.float32), second.astype(half), smooth.astype(half)


def kernel(
    bands, blocks,
    staves, weights, rep, win, length, first_in, twiddle_in, second_in, smooth_in,
    centroid, energy,
    xbuf, wbuf, sbuf, rbuf, fbuf, rhs, first, twiddle, second, smooth, near, acc, hrecv,
    xsem, wsem, csem, ssem, rsem, nsem, msem, hsem, gsem,
):
    me, block = lax.axis_index("band"), lax.axis_index("ping")
    each = wbuf.shape[0]

    loads = []
    for k in range(each):
        loads.append([
            pltpu.make_async_copy(staves.at[:, :, k], xbuf.at[k], xsem.at[k]),
            pltpu.make_async_copy(weights.at[:, k], wbuf.at[k], wsem.at[k]),
        ])
        for copy in loads[-1]:
            copy.start()
    consts = [
        pltpu.make_async_copy(a, b, csem.at[i])
        for i, (a, b) in enumerate([(first_in, first), (twiddle_in, twiddle), (second_in, second), (smooth_in, smooth)])
    ]
    for copy in consts:
        copy.start()

    near[...] = jnp.zeros_like(near)
    hrecv[...] = jnp.zeros_like(hrecv)

    barrier = pltpu.get_barrier_semaphore()

    @pl.loop(1, bands)
    def _(i):
        pl.semaphore_signal(barrier, inc=1, device_id={"band": lax.rem(me + i, bands)}, device_id_type=MESH)

    @pl.when(block > 0)
    def _():
        pl.semaphore_signal(barrier, inc=1, device_id={"ping": block - 1}, device_id_type=MESH)

    @pl.when(block < blocks - 1)
    def _():
        pl.semaphore_signal(barrier, inc=1, device_id={"ping": block + 1}, device_id_type=MESH)

    sides = (block > 0).astype(jnp.int32) + (block < blocks - 1).astype(jnp.int32)

    def beside(src, dst, up_sems, down_sems):
        up = pltpu.make_async_remote_copy(
            src, dst.at[0], up_sems.at[0], down_sems.at[0], device_id={"ping": block + 1}, device_id_type=MESH)
        down = pltpu.make_async_remote_copy(
            src, dst.at[1], up_sems.at[1], down_sems.at[1], device_id={"ping": block - 1}, device_id_type=MESH)
        return up, down

    def send(copies):
        @pl.when(block < blocks - 1)
        def _():
            copies[0].start()

        @pl.when(block > 0)
        def _():
            copies[1].start()

    def receive(copies):
        @pl.when(block > 0)
        def _():
            copies[0].wait_recv()

        @pl.when(block < blocks - 1)
        def _():
            copies[1].wait_recv()

    def sent(copies):
        @pl.when(block < blocks - 1)
        def _():
            copies[0].wait_send()

        @pl.when(block > 0)
        def _():
            copies[1].wait_send()

    edges = beside(win, near, nsem, msem)

    for k in range(each):
        for copy in loads[k]:
            copy.wait()
        x = xbuf[k].astype(jnp.float32).reshape(2 * 128, -1).astype(jnp.bfloat16)
        r0, r1 = rep[k, 0:1, :], rep[k, 1:2, :]
        columns = wbuf.shape[-1]
        width = 256
        for c in range(columns // width):
            here = pl.ds(c * width, width)
            p0 = jnp.dot(x, wbuf[k, 0, :, here], preferred_element_type=jnp.float32)
            p1 = jnp.dot(x, wbuf[k, 1, :, here], preferred_element_type=jnp.float32)
            re = (p0[:128] - p1[128:]).astype(jnp.bfloat16).T.astype(jnp.float32)
            im = (p1[:128] + p0[128:]).astype(jnp.bfloat16).T.astype(jnp.float32)
            cre = (re * r0 + im * r1).reshape(width // 8, 8, 128)
            cim = (im * r0 - re * r1).reshape(width // 8, 8, 128)
            sbuf[k, pl.ds(c * (width // 8), width // 8)] = jnp.concatenate([cre, cim], axis=1).astype(jnp.bfloat16)
        if k == 0:
            pl.semaphore_wait(barrier, bands - 1 + sides)
            send(edges)

        @pl.loop(1, bands)
        def _(i):
            other = lax.rem(me + i, bands)
            pltpu.make_async_remote_copy(
                sbuf.at[k, other], rbuf.at[k, me], ssem.at[k], rsem.at[k],
                device_id={"band": other}, device_id_type=MESH,
            ).start()

        rbuf[k, me] = sbuf[k, me]

    for k in range(each):
        pltpu.make_async_remote_copy(
            sbuf.at[k, pl.ds(0, bands - 1)], rbuf.at[k, pl.ds(0, bands - 1)], ssem.at[k], rsem.at[k],
            device_id={"band": lax.rem(me + 1, bands)}, device_id_type=MESH,
        ).wait_recv()
        fbuf[k] = rbuf[k].astype(jnp.float32).reshape(bands * 16, 128)

    for copy in consts:
        copy.wait()
    receive(edges)

    lane = lax.broadcasted_iota(jnp.int32, (16, 128), 1)
    wide = jnp.where(lane < 8 * REACH, near[1], jnp.where(lane >= 128 - 8 * REACH, near[0], 4096.0))
    near[0] = wide
    rows = lax.broadcasted_iota(jnp.int32, (SPLIT, 1), 0).astype(jnp.float32)

    @pl.loop(0, 4)
    def _(pair):
        for i in range(2):
            for j in range(each):
                for h in range(2):
                    part = fbuf[j, pl.ds(i * 8 + pair * 2 + h, bands, stride=16), :]
                    rhs[pl.ds((i * each + j) * bands, bands), h * 128 : (h + 1) * 128] = part.astype(jnp.bfloat16)
        y = jnp.dot(first[...], rhs[...], preferred_element_type=jnp.float32)
        for h in range(2):
            b = pair * 2 + h
            yr, yi = y[:SPLIT, h * 128 : (h + 1) * 128], y[SPLIT:, h * 128 : (h + 1) * 128]
            c, s = twiddle[0], twiddle[1]
            z = jnp.concatenate([yr * c - yi * s, yr * s + yi * c], axis=1).astype(jnp.bfloat16)
            w = jnp.dot(z, second[...], preferred_element_type=jnp.float32)
            wr, wi = w[:, :128], w[:, 128:]
            env = (wr * wr + wi * wi).astype(jnp.bfloat16)
            smoothed = jnp.dot(env, smooth[...], preferred_element_type=jnp.float32)
            for g in range(2):
                sm = smoothed[:, g * 128 : (g + 1) * 128]
                source = win if g == 0 else near.at[0]
                low, high = source[pl.ds(b, 1), :], source[pl.ds(b + 8, 1), :]
                v = jnp.where((rows >= low) & (rows < high), sm, 0.0)
                e = jnp.sum(v, axis=0, keepdims=True)
                m = jnp.sum(v * rows, axis=0, keepdims=True) + (0.5 - low) * e
                acc[g, pl.ds(b, 1), :] = e
                acc[g, pl.ds(b + 8, 1), :] = m

    partial = beside(acc.at[1], hrecv, hsem, gsem)
    send(partial)
    receive(partial)
    total = acc[0] + jnp.where(lane < 8 * REACH, hrecv[0], 0.0) + jnp.where(lane >= 128 - 8 * REACH, hrecv[1], 0.0)
    rowp = lax.broadcasted_iota(jnp.int32, (16, 128), 0)
    group = jnp.where(lane // 8 == rowp, 1.0, 0.0)
    both = lax.dot_general(
        group, total, (((1,), (1,)), ((), ())), precision=lax.Precision.HIGHEST, preferred_element_type=jnp.float32)
    place = block * 16 + lax.broadcasted_iota(jnp.int32, (16, 8), 0)
    weight = jnp.zeros((16, 8), jnp.float32)
    for j, tap in enumerate(TAPS):
        q = place + (j - REACH)
        weight = weight + jnp.where((q >= 0) & (q < blocks * 16), tap, 0.0)
    scale = (1.0 / (16.0 * SPLIT * BINS)) / weight
    e, m = both[:, :8] * scale, both[:, 8:] * scale
    widths = length[...]
    centroid[...] = m / (widths * (e + 1e-06))
    energy[...] = e / widths

    sent(edges)
    sent(partial)
    for k in range(each):
        pltpu.make_async_remote_copy(
            sbuf.at[k, pl.ds(0, bands - 1)], rbuf.at[k, pl.ds(0, bands - 1)], ssem.at[k], rsem.at[k],
            device_id={"band": lax.rem(me + 1, bands)}, device_id_type=MESH,
        ).wait_send()


def local(bands, blocks, staves, weights, replica, start, length):
    me = lax.axis_index("band")
    each = weights.shape[1]
    first, twiddle, second, smooth = tables(bands, each)
    own = lax.dynamic_slice_in_dim(replica, me * (each * BINS), each * BINS, axis=1)
    rep = jnp.broadcast_to(own.reshape(2, each, 1, BINS), (2, each, 16, BINS)).reshape(2, each, 128).swapaxes(0, 1)
    low = start.T.astype(jnp.float32)[:, :, None] - 256.0 * jnp.arange(8, dtype=jnp.float32)
    high = low + length.T.astype(jnp.float32)[:, :, None]
    win = jnp.concatenate([low.reshape(8, 128), high.reshape(8, 128)], axis=0)
    vmem, hbm = pl.BlockSpec(memory_space=pltpu.VMEM), pl.BlockSpec(memory_space=pl.ANY)
    f32, bf16, dma = jnp.float32, jnp.bfloat16, pltpu.SemaphoreType.DMA
    out = jax.ShapeDtypeStruct((16, 8), f32)
    return pl.pallas_call(
        functools.partial(kernel, bands, blocks),
        out_shape=(out, out),
        in_specs=[hbm, hbm, vmem, vmem, vmem, hbm, hbm, hbm, hbm],
        out_specs=(vmem, vmem),
        scratch_shapes=[
            pltpu.VMEM((each, 2, 16, 8, 512), bf16),
            pltpu.VMEM((each, 2, 512, 512), bf16),
            pltpu.VMEM((each, bands, 16, 128), bf16),
            pltpu.VMEM((each, bands, 16, 128), bf16),
            pltpu.VMEM((each, bands * 16, 128), f32),
            pltpu.VMEM((2 * each * bands, 256), bf16),
            pltpu.VMEM(first.shape, bf16),
            pltpu.VMEM(twiddle.shape, f32),
            pltpu.VMEM(second.shape, bf16),
            pltpu.VMEM(smooth.shape, bf16),
            pltpu.VMEM((2, 16, 128), f32),
            pltpu.VMEM((2, 16, 128), f32),
            pltpu.VMEM((2, 16, 128), f32),
            dma((each,)), dma((each,)), dma((4,)), dma((each,)), dma((each,)),
            dma((2,)), dma((2,)), dma((2,)), dma((2,)),
        ],
        compiler_params=pltpu.CompilerParams(collective_id=0, has_side_effects=True, vmem_limit_bytes=48 << 20),
    )(staves, weights, rep, win, length.astype(f32), first, twiddle, second, smooth)


def solution(mesh):
    in_specs = (
        P(None, "ping", "band", None, None),
        P(None, "band", None, None),
        P(),
        P("ping", "band"),
        P("ping", "band"),
    )
    out_specs = (P("ping", "band"), P("ping", "band"))
    step = functools.partial(local, mesh.shape["band"], mesh.shape["ping"])
    return jax.shard_map(step, mesh=mesh, in_specs=in_specs, out_specs=out_specs, check_vma=False)
```

time: 431 us -> 55.4 us (0.13); the launches traced: 426 us -> 55 us
  matrix products: 259 us -> 0 us
  local copies, waits for them, and re-layouts: 106 us -> 8.52 us
  Pallas kernels: 0 us -> 45 us
  waiting for transfers between devices: 32.2 us -> 0 us
  starting transfers between devices: 25.2 us -> 0 us
    dot_general x8 -> x0, matrix products: 259 us -> none  [the longest x1 63 us: envelope_rows(): jnp.dot(comp_re, sin_table, preferred_element_type=jnp.float32)]
    pallas_call x0 -> x1, Pallas kernels: none -> 45 us  [local(): pl.pallas_call(functools.partial(kernel, bands, blocks), out_shape=(out,...]
    convert_element_type x5 -> x1, local copies, waits for them, and re-layouts: 42.2 us -> 0.07 us  [local(): high = low + length.T.astype(jnp.float32)[:, :, None]]
    all_to_all x2 -> x0, local copies, waits for them, and re-layouts: 28.9 us -> none  [local(): lax.all_to_all(beams, 'band', split_axis=4, concat_axis=1, tiled=True)]
    all_to_all x1 -> x0, waiting for transfers between devices: 27.5 us -> none  [local(): lax.all_to_all(beams, 'band', split_axis=4, concat_axis=1, tiled=True)]
    all_to_all x1 -> x0, starting transfers between devices: 15.9 us -> none  [local(): lax.all_to_all(beams, 'band', split_axis=4, concat_axis=1, tiled=True)]
    unnamed x12 -> x13, local copies, waits for them, and re-layouts: 21.5 us -> 6.42 us
    another operation x1 -> x0, local copies, waits for them, and re-layouts: 12.1 us -> none  [local(): beams = jnp.stack([beam_re, beam_im]).astype(jnp.bfloat16)]
  transfers between devices with their start and end apart: 3 -> 0, of which waited for: 3 -> 0; matrix products, arithmetic and copies ran while one was open for 0% -> 0% of each run, Pallas kernels for 0% -> 0%
where the time goes in v1:
time: 55.4 us; the launch traced here: 55 us
  Pallas kernels  45 us (81%)
  local copies, waits for them, and re-layouts  8.52 us (15%)
  other arithmetic  0.72 us (1%)
  between operations  0.71 us (1%)
    pallas_call x1, Pallas kernels, local(): pl.pallas_call(functools.partial(kernel, bands, blocks), out_shape=(out,...  45 us
    unnamed x13, local copies, waits for them, and re-layouts  6.42 us
    pallas_call x2, local copies, waits for them, and re-layouts, local(): pl.pallas_call(functools.partial(kernel, bands, blocks), out_shape=(out,...  1.32 us

profile of v1, /device:TPU:1, one launch (start us, length us, event | category | flops | bytes accessed | tf_op | source)
XLA Modules:
  0.0 55.0 jit_solution(10324561719275197125)
XLA Ops:
  0.6 0.0 copy-start
  0.6 0.7 %copy-done = f32[2,2048]{1,0:T(2,128)S(1)} copy-done((f32[2,2048]{1,0:T(2,128)S(1)}, f32[2,2048]{1,0:T(2,128)}, u32[]{:S(2)}) %copy-start) | copy-done | bytes 16408
  1.4 0.1 constant_dynamic-slice_fusion
  1.4 0.1 broadcast_in_dim.4
  1.5 0.1 reshape.22
  1.6 0.8 %copy.17 = s32[16,8]{1,0:T(8,128)S(1)} copy(s32[16,8]{0,1:T(8,128)} %param.13) | data formatting | bytes 1024 | tf_op args[4]
  2.4 0.1 copy.18
  2.5 0.1 add.15
  2.5 0.1 add.16
  2.6 0.7 %convert_bitcast_fusion = f32[8,16]{1,0:T(8,128)S(1)} fusion(s32[16,8]{0,1:T(8,128)} %param.12), kind=kLoop, calls=%fused_computation.2 | loop fusion | flops 128 | bytes 1024 | tf_op jit(solution)/shard_map/convert_element_type | solution.py:230
  3.3 0.1 sub.21
  3.4 0.1 sub.22
  3.5 0.1 sub.24
  3.7 0.0 copy-start.1
  3.7 1.2 %copy-done.1 = bf16[2,16,4,8,512]{4,3,2,1,0:T(8,128)(2,1)S(1)} copy-done((bf16[2,16,4,8,512]{4,3,2,1,0:T(8,128)(2,1)S(1)}, bf16[2,16,4,8,512]{4,3,2,1,0:T(8,128)(2,1)}, u32[]{:S(2)}) %copy-start.1) | copy-done | bytes 1048600
  4.9 0.0 copy-start.2
  4.9 1.0 %copy-done.2 = bf16[512,512]{1,0:T(8,128)(2,1)S(1)} copy-done((bf16[512,512]{1,0:T(8,128)(2,1)S(1)}, bf16[512,512]{1,0:T(8,128)(2,1)}, u32[]{:S(2)}) %copy-start.2) | copy-done | bytes 524312
  5.9 0.0 copy-start.3
  5.9 0.9 %copy-done.3 = f32[2,256,128]{2,1,0:T(8,128)S(1)} copy-done((f32[2,256,128]{2,1,0:T(8,128)S(1)}, f32[2,256,128]{2,1,0:T(8,128)}, u32[]{:S(2)}) %copy-start.3) | copy-done | bytes 262168
  6.9 0.0 copy-start.4
  6.9 0.9 %copy-done.4 = bf16[256,256]{1,0:T(8,128)(2,1)S(1)} copy-done((bf16[256,256]{1,0:T(8,128)(2,1)S(1)}, bf16[256,256]{1,0:T(8,128)(2,1)}, u32[]{:S(2)}) %copy-start.4) | copy-done | bytes 131096
  7.8 0.0 copy-start.5
  7.8 0.8 %copy-done.5 = bf16[128,256]{1,0:T(8,128)(2,1)S(1)} copy-done((bf16[128,256]{1,0:T(8,128)(2,1)S(1)}, bf16[128,256]{1,0:T(8,128)(2,1)}, u32[]{:S(2)}) %copy-start.5) | copy-done | bytes 65560
  8.6 45.0 %shard_map.104 = (f32[16,8]{1,0:T(8,128)S(1)}, f32[16,8]{1,0:T(8,128)S(1)}) custom-call(bf16[2,16,4,8,512]{4,3,2,1,0:T(8,128)(2,1)S(1)} %copy-done.1, bf16[2,4,512,512]{3,2,1,0:T(8,128)(2,1)} %weights.1, f32[4,2,128]{2,1,0:T(2,128)S(1)} %bitcast.9, f32[16,128]{1,0:T(8,128)S(1)} %pad_maximum_fusion.win, f32[16,8]{1,0:T(8,128)S(1)} %get-tuple-element.8.length, ...), custom_call_target="tpu_custom_call" | custom-call | tf_op jit(solution)/shard_map/pallas_call | solution.py:236
  53.7 0.7 %copy.19 = f32[16,8]{0,1:T(8,128)} copy(f32[16,8]{1,0:T(8,128)S(1)} %get-tuple-element.4) | data formatting | bytes 1024 | tf_op jit(solution)/shard_map/pallas_call | solution.py:236
  54.3 0.7 %copy.20 = f32[16,8]{0,1:T(8,128)} copy(f32[16,8]{1,0:T(8,128)S(1)} %get-tuple-element.5) | data formatting | bytes 1024 | tf_op jit(solution)/shard_map/pallas_call | solution.py:236
  (7 shorter events, 0.0 us)
Async XLA Ops:
  0.6 0.7 %copy-start = (f32[2,2048]{1,0:T(2,128)S(1)}, f32[2,2048]{1,0:T(2,128)}, u32[]{:S(2)}) copy-start(f32[2,2048]{1,0:T(2,128)} %param.11) | copy-start | bytes 49156
  3.7 1.2 %copy-start.1 = (bf16[2,16,4,8,512]{4,3,2,1,0:T(8,128)(2,1)S(1)}, bf16[2,16,4,8,512]{4,3,2,1,0:T(8,128)(2,1)}, u32[]{:S(2)}) copy-start(bf16[2,16,4,8,512]{4,3,2,1,0:T(8,128)(2,1)} %staves.1) | copy-start | bytes 3145732
  4.9 1.0 %copy-start.2 = (bf16[512,512]{1,0:T(8,128)(2,1)S(1)}, bf16[512,512]{1,0:T(8,128)(2,1)}, u32[]{:S(2)}) copy-start(bf16[512,512]{1,0:T(8,128)(2,1)} %constant.20.clone.first_in) | copy-start | bytes 1572868
  5.9 0.9 %copy-start.3 = (f32[2,256,128]{2,1,0:T(8,128)S(1)}, f32[2,256,128]{2,1,0:T(8,128)}, u32[]{:S(2)}) copy-start(f32[2,256,128]{2,1,0:T(8,128)} %constant.21.clone.twiddle_in) | copy-start | bytes 786436
  6.9 0.9 %copy-start.4 = (bf16[256,256]{1,0:T(8,128)(2,1)S(1)}, bf16[256,256]{1,0:T(8,128)(2,1)}, u32[]{:S(2)}) copy-start(bf16[256,256]{1,0:T(8,128)(2,1)} %constant.22.clone.second_in) | copy-start | bytes 393220
  7.8 0.8 %copy-start.5 = (bf16[128,256]{1,0:T(8,128)(2,1)S(1)}, bf16[128,256]{1,0:T(8,128)(2,1)}, u32[]{:S(2)}) copy-start(bf16[128,256]{1,0:T(8,128)(2,1)} %constant.23.clone.smooth_in) | copy-start | bytes 196612

commit v2 on v1

--- a/solution.py
+++ b/solution.py
@@ -42,14 +42,20 @@
 
 def kernel(
     bands, blocks,
-    staves, weights, rep, win, length, first_in, twiddle_in, second_in, smooth_in,
+    staves, weights, replica, start, length, first_in, twiddle_in, second_in, smooth_in,
     centroid, energy,
-    xbuf, wbuf, sbuf, rbuf, fbuf, rhs, first, twiddle, second, smooth, near, acc, hrecv,
-    xsem, wsem, csem, ssem, rsem, nsem, msem, hsem, gsem,
+    qbuf, tbuf, rep, win, xbuf, wbuf, sbuf, rbuf, fbuf, rhs, first, twiddle, second, smooth, near, acc, hrecv,
+    qsem, xsem, wsem, csem, ssem, rsem, nsem, msem, hsem, gsem,
 ):
     me, block = lax.axis_index("band"), lax.axis_index("ping")
     each = wbuf.shape[0]
 
+    small = [
+        pltpu.make_async_copy(a, b, qsem.at[i])
+        for i, (a, b) in enumerate([(replica, qbuf), (start, tbuf.at[0]), (length, tbuf.at[1])])
+    ]
+    for copy in small:
+        copy.start()
     loads = []
     for k in range(each):
         loads.append([
@@ -119,6 +125,23 @@
             copies[1].wait_send()
 
     edges = beside(win, near, nsem, msem)
+
+    for copy in small:
+        copy.wait()
+    span = each * BINS
+    spread = functools.partial(jnp.dot, precision=lax.Precision.HIGHEST, preferred_element_type=jnp.float32)
+    row, column = (lax.broadcasted_iota(jnp.int32, (128, 128), d) for d in (0, 1))
+    per_tile = 128 // span
+    part = qbuf[:, pl.ds(pl.multiple_of(lax.div(me, per_tile) * 128, 128), 128)]
+    for k in range(each):
+        pick = jnp.where(row == lax.rem(me, per_tile) * span + k * BINS + lax.rem(column, BINS), 1.0, 0.0)
+        rep[k] = spread(part, pick)
+    row, column = (lax.broadcasted_iota(jnp.int32, (16, 128), d) for d in (0, 1))
+    pick = jnp.where(row == lax.div(column, BINS), 1.0, 0.0)
+    times = spread(tbuf[...].astype(jnp.float32).reshape(16, 16), pick)
+    low = times[:8] - (lax.rem(column[:8], BINS) * SPLIT).astype(jnp.float32)
+    win[0:8] = low
+    win[8:16] = low + times[8:]
 
     for k in range(each):
         for copy in loads[k]:
@@ -200,15 +223,15 @@
     rowp = lax.broadcasted_iota(jnp.int32, (16, 128), 0)
     group = jnp.where(lane // 8 == rowp, 1.0, 0.0)
     both = lax.dot_general(
-        group, total, (((1,), (1,)), ((), ())), precision=lax.Precision.HIGHEST, preferred_element_type=jnp.float32)
-    place = block * 16 + lax.broadcasted_iota(jnp.int32, (16, 8), 0)
-    weight = jnp.zeros((16, 8), jnp.float32)
+        total, group, (((1,), (1,)), ((), ())), precision=lax.Precision.HIGHEST, preferred_element_type=jnp.float32)
+    place = block * 16 + lax.broadcasted_iota(jnp.int32, (8, 16), 1)
+    weight = jnp.zeros((8, 16), jnp.float32)
     for j, tap in enumerate(TAPS):
         q = place + (j - REACH)
         weight = weight + jnp.where((q >= 0) & (q < blocks * 16), tap, 0.0)
     scale = (1.0 / (16.0 * SPLIT * BINS)) / weight
-    e, m = both[:, :8] * scale, both[:, 8:] * scale
-    widths = length[...]
+    e, m = both[:8] * scale, both[8:] * scale
+    widths = tbuf[1].astype(jnp.float32)
     centroid[...] = m / (widths * (e + 1e-06))
     energy[...] = e / widths
 
@@ -222,23 +245,21 @@
 
 
 def local(bands, blocks, staves, weights, replica, start, length):
-    me = lax.axis_index("band")
     each = weights.shape[1]
     first, twiddle, second, smooth = tables(bands, each)
-    own = lax.dynamic_slice_in_dim(replica, me * (each * BINS), each * BINS, axis=1)
-    rep = jnp.broadcast_to(own.reshape(2, each, 1, BINS), (2, each, 16, BINS)).reshape(2, each, 128).swapaxes(0, 1)
-    low = start.T.astype(jnp.float32)[:, :, None] - 256.0 * jnp.arange(8, dtype=jnp.float32)
-    high = low + length.T.astype(jnp.float32)[:, :, None]
-    win = jnp.concatenate([low.reshape(8, 128), high.reshape(8, 128)], axis=0)
-    vmem, hbm = pl.BlockSpec(memory_space=pltpu.VMEM), pl.BlockSpec(memory_space=pl.ANY)
+    vmem, hbm = pl.BlockSpec(memory_space=pltpu.VMEM), pl.BlockSpec(memory_space=pltpu.HBM)
     f32, bf16, dma = jnp.float32, jnp.bfloat16, pltpu.SemaphoreType.DMA
-    out = jax.ShapeDtypeStruct((16, 8), f32)
-    return pl.pallas_call(
+    out = jax.ShapeDtypeStruct((8, 16), f32)
+    centroid, energy = pl.pallas_call(
         functools.partial(kernel, bands, blocks),
         out_shape=(out, out),
-        in_specs=[hbm, hbm, vmem, vmem, vmem, hbm, hbm, hbm, hbm],
+        in_specs=[hbm] * 9,
         out_specs=(vmem, vmem),
         scratch_shapes=[
+            pltpu.VMEM(replica.shape, f32),
+            pltpu.VMEM((2, 8, 16), jnp.int32),
+            pltpu.VMEM((each, 2, 128), f32),
+            pltpu.VMEM((16, 128), f32),
             pltpu.VMEM((each, 2, 16, 8, 512), bf16),
             pltpu.VMEM((each, 2, 512, 512), bf16),
             pltpu.VMEM((each, bands, 16, 128), bf16),
@@ -252,11 +273,12 @@
             pltpu.VMEM((2, 16, 128), f32),
             pltpu.VMEM((2, 16, 128), f32),
             pltpu.VMEM((2, 16, 128), f32),
-            dma((each,)), dma((each,)), dma((4,)), dma((each,)), dma((each,)),
+            dma((3,)), dma((each,)), dma((each,)), dma((4,)), dma((each,)), dma((each,)),
             dma((2,)), dma((2,)), dma((2,)), dma((2,)),
         ],
-        compiler_params=pltpu.CompilerParams(collective_id=0, has_side_effects=True, vmem_limit_bytes=48 << 20),
-    )(staves, weights, rep, win, length.astype(f32), first, twiddle, second, smooth)
+        compiler_params=pltpu.CompilerParams(collective_id=0, has_side_effects=True, vmem_limit_bytes=63 << 20),
+    )(staves, weights, replica, start.T, length.T, first, twiddle, second, smooth)
+    return centroid.T, energy.T
 
 
 def solution(mesh):

time: 55.4 us -> 48.9 us (0.88)
  local copies, waits for them, and re-layouts: 8.52 us -> 2.53 us
  other arithmetic: 0.72 us -> 0 us
  Pallas kernels: 45 us -> 45.6 us
    unnamed x13 -> x2, local copies, waits for them, and re-layouts: 6.42 us -> 2.53 us
    pallas_call x2 -> x0, local copies, waits for them, and re-layouts: 1.32 us -> none  [local(): pl.pallas_call(functools.partial(kernel, bands, blocks), out_shape=(out,...]
    convert_element_type x2 -> x0, other arithmetic: 0.7 us -> none  [the longest x1 0.69 us: local(): start.T.astype(jnp.float32)[:, :, None]]
    pallas_call x1, Pallas kernels: 45 us -> 45.6 us  [local(): pl.pallas_call(functools.partial(kernel, bands, blocks), out_shape=(out,...]
where the time goes in v2:
time: 48.9 us; the launch traced here: 48.8 us
  Pallas kernels  45.6 us (93%)
  local copies, waits for them, and re-layouts  2.53 us (5%)
  between operations  0.64 us (1%)
    pallas_call x1, Pallas kernels, local(): pl.pallas_call(functools.partial(kernel, bands, blocks), out_shape=(out,...  45.6 us
    unnamed x2, local copies, waits for them, and re-layouts  2.53 us

profile of v2, /device:TPU:1, one launch (start us, length us, event | category | flops | bytes accessed | tf_op | source)
XLA Modules:
  0.0 48.8 jit_solution(181496261092208610)
XLA Ops:
  0.6 45.6 %shard_map.104 = (f32[8,16]{1,0:T(8,128)}, f32[8,16]{1,0:T(8,128)}) custom-call(bf16[2,16,4,8,512]{4,3,2,1,0:T(8,128)(2,1)} %staves.1, bf16[2,4,512,512]{3,2,1,0:T(8,128)(2,1)} %weights.1, f32[2,2048]{1,0:T(2,128)} %replica.1, s32[8,16]{1,0:T(8,128)} %bitcast.4, s32[8,16]{1,0:T(8,128)} %bitcast.5, bf16[512,512]{1,0:T(8,128)(2,1)} %constant.8.clone.first_in, ...), custom_call_target="tpu_custom_call" | custom-call | tf_op jit(solution)/shard_map/pallas_call | solution.py:253
  46.2 1.3 %copy.13 = f32[16,8]{0,1:T(8,128)} copy(f32[16,8]{0,1:T(8,128)} %bitcast.7) | data formatting | bytes 1024
  47.5 1.3 %copy.14 = f32[16,8]{0,1:T(8,128)} copy(f32[16,8]{0,1:T(8,128)} %bitcast.6) | data formatting | bytes 1024

commit v3 on v2

v3 whole, which is shorter than its diff:
```python
import functools
import math

import ml_dtypes
import numpy as np

import jax
import jax.numpy as jnp
from jax import lax
from jax.experimental import pallas as pl
from jax.experimental.pallas import tpu as pltpu
from jax.sharding import PartitionSpec as P

MESH = pl.DeviceIdType.MESH
BINS, SPLIT, REACH = 8, 256, 4
ROW = 8
TAPS = (1.0, 2.0, 3.0, 4.0, 5.0, 4.0, 3.0, 2.0, 1.0)


def tables(sources, bands_each):
    total = SPLIT * BINS
    turn = 2.0 * math.pi / total
    t1 = np.arange(SPLIT)
    half_of, plane = np.divmod(np.arange(sources), sources // 2)
    source = (plane // ROW * 2 + half_of) * ROW + plane % ROW
    band = (source[None, :] * bands_each + np.arange(bands_each)[:, None]).reshape(-1)
    angle = ((t1[:, None] * band[None, :] * BINS) % total) * turn
    first = np.block([[np.cos(angle), -np.sin(angle)], [np.sin(angle), np.cos(angle)]])
    lane = np.arange(128)
    ping, small = lane // BINS, lane % BINS
    angle = ((t1[:, None] * small[None, :]) % total) * turn
    twiddle = np.stack([np.cos(angle), np.sin(angle)])
    same = ping[:, None] == ping[None, :]
    angle = ((small[:, None] * small[None, :]) % BINS) * (2.0 * math.pi / BINS)
    cos, sin = np.cos(angle) * same, np.sin(angle) * same
    second = np.block([[cos, sin], [-sin, cos]])
    above, below = ping + 16, ping - 16
    beside = np.where(ping < REACH, above, np.where(ping >= 16 - REACH, below, 1000))
    target = np.concatenate([ping, beside])
    kind = np.concatenate([small, small])
    smooth = np.maximum(5 - np.abs(ping[:, None] - target[None, :]), 0) * (small[:, None] == kind[None, :])
    half = ml_dtypes.bfloat16
    return first.astype(half), twiddle.astype(np.float32), second.astype(half), smooth.astype(half)


def kernel(
    bands, blocks,
    staves, weights, replica, start, length, first_in, twiddle_in, second_in, smooth_in,
    result,
    qbuf, tbuf, rep, win, xbuf, wbuf, sbuf, over, gathered, plane, beyond, fbuf, rhs, ebuf,
    first, twiddle, second, smooth, near, acc, hrecv,
    qsem, xsem, wsem, csem, psend, precv, zsend, zrecv, nsem, msem, hsem, gsem,
):
    me, block = lax.axis_index("band"), lax.axis_index("ping")
    each = wbuf.shape[0]
    columns = bands // (2 * ROW)
    here_z = lax.rem(lax.div(me, ROW), 2)
    there_z = 1 - here_z
    y, r = lax.div(me, 2 * ROW), lax.rem(me, ROW)
    mine = y * ROW + r

    def at(y, z, r):
        return {"band": (y * 2 + z) * ROW + r}

    near[...] = jnp.zeros_like(near)
    hrecv[...] = jnp.zeros_like(hrecv)

    barrier = pltpu.get_barrier_semaphore()
    pl.semaphore_signal(barrier, inc=1, device_id=at(y, there_z, r), device_id_type=MESH)

    @pl.loop(1, columns * ROW)
    def _(i):
        place = lax.rem(mine + i, columns * ROW)
        pl.semaphore_signal(
            barrier, inc=1, device_id=at(lax.div(place, ROW), here_z, lax.rem(place, ROW)), device_id_type=MESH)

    @pl.when(block > 0)
    def _():
        pl.semaphore_signal(barrier, inc=1, device_id={"ping": block - 1}, device_id_type=MESH)

    @pl.when(block < blocks - 1)
    def _():
        pl.semaphore_signal(barrier, inc=1, device_id={"ping": block + 1}, device_id_type=MESH)

    loads = []
    for k in range(each):
        loads.append([
            pltpu.make_async_copy(staves.at[:, :, k], xbuf.at[k], xsem.at[k]),
            pltpu.make_async_copy(weights.at[:, k], wbuf.at[k], wsem.at[k]),
        ])
        for copy in loads[-1]:
            copy.start()
        if k == 0:
            small = [
                pltpu.make_async_copy(a, b, qsem.at[i])
                for i, (a, b) in enumerate([(replica, qbuf), (start, tbuf.at[0]), (length, tbuf.at[1])])
            ]
            for copy in small:
                copy.start()
    consts = [
        pltpu.make_async_copy(a, b, csem.at[i])
        for i, (a, b) in enumerate([(first_in, first), (twiddle_in, twiddle), (second_in, second), (smooth_in, smooth)])
    ]
    for copy in consts:
        copy.start()

    def across(src, dst, n):
        return pltpu.make_async_remote_copy(
            src, dst, zsend.at[n], zrecv.at[n], device_id=at(y, there_z, r), device_id_type=MESH)

    size = columns * ROW

    def scatter(src, dst, n):
        @pl.loop(1, size)
        def _(i):
            place = lax.rem(mine + i, size)
            pltpu.make_async_remote_copy(
                src.at[place], dst.at[mine], psend.at[n], precv.at[n],
                device_id=at(lax.div(place, ROW), here_z, lax.rem(place, ROW)), device_id_type=MESH,
            ).start()

        dst[mine] = src[mine]

    def scattered(src, dst, n):
        rest = pl.ds(0, size - 1)
        return pltpu.make_async_remote_copy(
            src.at[rest], dst.at[rest], psend.at[n], precv.at[n],
            device_id=at(y, here_z, lax.rem(r + 1, ROW)), device_id_type=MESH)

    sides = (block > 0).astype(jnp.int32) + (block < blocks - 1).astype(jnp.int32)

    def beside(src, dst, up_sems, down_sems):
        up = pltpu.make_async_remote_copy(
            src, dst.at[0], up_sems.at[0], down_sems.at[0], device_id={"ping": block + 1}, device_id_type=MESH)
        down = pltpu.make_async_remote_copy(
            src, dst.at[1], up_sems.at[1], down_sems.at[1], device_id={"ping": block - 1}, device_id_type=MESH)
        return up, down

    def send(copies):
        @pl.when(block < blocks - 1)
        def _():
            copies[0].start()

        @pl.when(block > 0)
        def _():
            copies[1].start()

    def receive(copies):
        @pl.when(block > 0)
        def _():
            copies[0].wait_recv()

        @pl.when(block < blocks - 1)
        def _():
            copies[1].wait_recv()

    def sent(copies):
        @pl.when(block < blocks - 1)
        def _():
            copies[0].wait_send()

        @pl.when(block > 0)
        def _():
            copies[1].wait_send()

    edges = beside(win, near, nsem, msem)

    for copy in small:
        copy.wait()
    span = each * BINS
    spread = functools.partial(jnp.dot, precision=lax.Precision.HIGHEST, preferred_element_type=jnp.float32)
    row, column = (lax.broadcasted_iota(jnp.int32, (128, 128), d) for d in (0, 1))
    per_tile = 128 // span
    part = qbuf[:, pl.ds(pl.multiple_of(lax.div(me, per_tile) * 128, 128), 128)]
    for k in range(each):
        pick = jnp.where(row == lax.rem(me, per_tile) * span + k * BINS + lax.rem(column, BINS), 1.0, 0.0)
        rep[k] = spread(part, pick)
    row, column = (lax.broadcasted_iota(jnp.int32, (16, 128), d) for d in (0, 1))
    pick = jnp.where(row == lax.div(column, BINS), 1.0, 0.0)
    times = spread(tbuf[...].astype(jnp.float32).reshape(16, 16), pick)
    low = times[:8] - (lax.rem(column[:8], BINS) * SPLIT).astype(jnp.float32)
    win[0:8] = low
    win[8:16] = low + times[8:]

    def beams(k, c):
        x = xbuf[k].astype(jnp.float32).reshape(2 * 128, -1).astype(jnp.bfloat16)
        r0, r1 = rep[k, 0:1, :], rep[k, 1:2, :]
        here = pl.ds(c * 256, 256)
        p0 = jnp.dot(x, wbuf[k, 0, :, here], preferred_element_type=jnp.float32)
        p1 = jnp.dot(x, wbuf[k, 1, :, here], preferred_element_type=jnp.float32)
        re = (p0[:128] - p1[128:]).astype(jnp.bfloat16).T.astype(jnp.float32)
        im = (p1[:128] + p0[128:]).astype(jnp.bfloat16).T.astype(jnp.float32)
        return (re * r0 + im * r1).reshape(32, 8, 128), (im * r0 - re * r1).reshape(32, 8, 128)

    def put(n, c, parts):
        tiles = jnp.concatenate(parts, axis=1).astype(jnp.bfloat16)
        for i in range(4):
            sbuf[n, i % 2, (c * 2 + i // 2) * ROW : (c * 2 + i // 2 + 1) * ROW] = tiles[i * ROW : (i + 1) * ROW]

    chunks = wbuf.shape[-1] // 256

    def early(k):
        for copy in loads[k]:
            copy.wait()
        for c in range(chunks):
            put(k, c, beams(k, c))

    early(0)
    pl.semaphore_wait(barrier, size + sides)
    across(sbuf.at[0, there_z], over.at[0], 0).start()
    send(edges)
    for k in (2, 3):
        for copy in loads[k]:
            copy.wait()
    for c in range(chunks):
        a, b = beams(2, c), beams(3, c)
        for h in range(2):
            part = slice(4 * h, 4 * h + 4)
            put(2 + h, c, [a[0][:, part], b[0][:, part], a[1][:, part], b[1][:, part]])
    for h in range(2):
        scatter(sbuf.at[2 + h, there_z], gathered.at[h], 4 + h)
    early(1)
    across(sbuf.at[1, there_z], over.at[1], 1).start()

    scattered(sbuf.at[2, there_z], gathered.at[0], 4).wait_recv()
    across(gathered.at[0], beyond.at[2], 2).start()
    for n in range(3):
        scatter(sbuf.at[n, here_z], plane.at[n], n)
    across(sbuf.at[0, there_z], over.at[0], 0).wait_recv()
    scatter(over.at[0], beyond.at[0], 6)
    scatter(sbuf.at[3, here_z], plane.at[3], 3)
    scattered(sbuf.at[3, there_z], gathered.at[1], 5).wait_recv()
    across(sbuf.at[1, there_z], over.at[1], 1).wait_recv()
    across(gathered.at[1], beyond.at[3], 3).start()
    scatter(over.at[1], beyond.at[1], 7)

    half = columns * ROW * 16

    def unpack(n, z, tiles):
        fbuf[n, pl.ds(z * half, half)] = tiles.astype(jnp.float32).reshape(half, 128)

    for copy in consts:
        copy.wait()
    receive(edges)
    lane = lax.broadcasted_iota(jnp.int32, (16, 128), 1)
    wide = jnp.where(lane < 8 * REACH, near[1], jnp.where(lane >= 128 - 8 * REACH, near[0], 4096.0))
    near[0] = wide
    rows = lax.broadcasted_iota(jnp.int32, (SPLIT, 1), 0).astype(jnp.float32)

    for k in range(2):
        scattered(sbuf.at[k, here_z], plane.at[k], k).wait_recv()
        unpack(k, here_z, plane[k])
        scattered(over.at[k], beyond.at[k], 6 + k).wait_recv()
        unpack(k, there_z, beyond[k])

    def window(b, g):
        sm = jnp.dot(ebuf[b], smooth[:, g * 128 : (g + 1) * 128], preferred_element_type=jnp.float32)
        source = win if g == 0 else near.at[0]
        low, high = source[pl.ds(b, 1), :], source[pl.ds(b + 8, 1), :]
        v = jnp.where((rows >= low) & (rows < high), sm, 0.0)
        e = jnp.sum(v, axis=0, keepdims=True)
        m = jnp.sum(v * rows, axis=0, keepdims=True) + (0.5 - low) * e
        acc[g, pl.ds(b, 1), :] = e
        acc[g, pl.ds(b + 8, 1), :] = m

    def transform(half_of, pair):
        for i in range(2):
            for j in range(4):
                for h in range(2):
                    q = pair * 2 + h
                    n, at_row = (j, half_of * 4 + q) if j < 2 else (2 + half_of, (j - 2) * 4 + q)
                    part = fbuf[n, pl.ds(i * 8 + at_row, bands, stride=16), :]
                    rhs[pl.ds((i * each + j) * bands, bands), h * 128 : (h + 1) * 128] = part.astype(jnp.bfloat16)
        out = jnp.dot(first[...], rhs[...], preferred_element_type=jnp.float32)
        for h in range(2):
            re, im = out[:SPLIT, h * 128 : (h + 1) * 128], out[SPLIT:, h * 128 : (h + 1) * 128]
            c, s = twiddle[0], twiddle[1]
            z = jnp.concatenate([re * c - im * s, re * s + im * c], axis=1).astype(jnp.bfloat16)
            w = jnp.dot(z, second[...], preferred_element_type=jnp.float32)
            wr, wi = w[:, :128], w[:, 128:]
            ebuf[half_of * 4 + pair * 2 + h] = (wr * wr + wi * wi).astype(jnp.bfloat16)
            window(half_of * 4 + pair * 2 + h, 1)

    partial = beside(acc.at[1], hrecv, hsem, gsem)
    for h in range(2):
        scattered(sbuf.at[2 + h, here_z], plane.at[2 + h], 2 + h).wait_recv()
        unpack(2 + h, here_z, plane[2 + h])
        across(gathered.at[h], beyond.at[2 + h], 2 + h).wait_recv()
        unpack(2 + h, there_z, beyond[2 + h])

        @pl.loop(0, 2)
        def _(pair):
            transform(h, pair)

        if h == 1:
            send(partial)

        @pl.loop(0, 4)
        def _(q):
            window(h * 4 + q, 0)

    receive(partial)
    total = acc[0] + jnp.where(lane < 8 * REACH, hrecv[0], 0.0) + jnp.where(lane >= 128 - 8 * REACH, hrecv[1], 0.0)
    rowp = lax.broadcasted_iota(jnp.int32, (16, 128), 0)
    group = jnp.where(lane // 8 == rowp, 1.0, 0.0)
    both = lax.dot_general(
        total, group, (((1,), (1,)), ((), ())), precision=lax.Precision.HIGHEST, preferred_element_type=jnp.float32)
    place = block * 16 + lax.broadcasted_iota(jnp.int32, (8, 16), 1)
    weight = jnp.zeros((8, 16), jnp.float32)
    for j, tap in enumerate(TAPS):
        q = place + (j - REACH)
        weight = weight + jnp.where((q >= 0) & (q < blocks * 16), tap, 0.0)
    scale = (1.0 / (16.0 * SPLIT * BINS)) / weight
    e, m = both[:8] * scale, both[8:] * scale
    widths = tbuf[1].astype(jnp.float32)
    result[0] = m / (widths * (e + 1e-06))
    result[1] = e / widths

    sent(edges)
    sent(partial)
    for k in range(2):
        scattered(sbuf.at[k, here_z], plane.at[k], k).wait_send()
        scattered(sbuf.at[2 + k, here_z], plane.at[2 + k], 2 + k).wait_send()
        scattered(sbuf.at[2 + k, there_z], gathered.at[k], 4 + k).wait_send()
        scattered(over.at[k], beyond.at[k], 6 + k).wait_send()
        across(sbuf.at[k, there_z], over.at[k], k).wait_send()
        across(gathered.at[k], beyond.at[2 + k], 2 + k).wait_send()


def local(bands, blocks, staves, weights, replica, start, length):
    each = weights.shape[1]
    first, twiddle, second, smooth = tables(bands, each)
    vmem, hbm = pl.BlockSpec(memory_space=pltpu.VMEM), pl.BlockSpec(memory_space=pltpu.HBM)
    f32, bf16, dma = jnp.float32, jnp.bfloat16, pltpu.SemaphoreType.DMA
    plane = (bands // 2, 16, 128)
    out = pl.pallas_call(
        functools.partial(kernel, bands, blocks),
        out_shape=jax.ShapeDtypeStruct((2, 8, 16), f32),
        in_specs=[hbm] * 9,
        out_specs=vmem,
        scratch_shapes=[
            pltpu.VMEM(replica.shape, f32),
            pltpu.VMEM((2, 8, 16), jnp.int32),
            pltpu.VMEM((each, 2, 128), f32),
            pltpu.VMEM((16, 128), f32),
            pltpu.VMEM((each, 2, 16, 8, 512), bf16),
            pltpu.VMEM((each, 2, 512, 512), bf16),
            pltpu.VMEM((each, 2, *plane), bf16),
            pltpu.VMEM((2, *plane), bf16),
            pltpu.VMEM((2, *plane), bf16),
            pltpu.VMEM((each, *plane), bf16),
            pltpu.VMEM((each, *plane), bf16),
            pltpu.VMEM((each, bands * 16, 128), f32),
            pltpu.VMEM((2 * each * bands, 256), bf16),
            pltpu.VMEM((8, SPLIT, 128), bf16),
            pltpu.VMEM(first.shape, bf16),
            pltpu.VMEM(twiddle.shape, f32),
            pltpu.VMEM(second.shape, bf16),
            pltpu.VMEM(smooth.shape, bf16),
            pltpu.VMEM((2, 16, 128), f32),
            pltpu.VMEM((2, 16, 128), f32),
            pltpu.VMEM((2, 16, 128), f32),
            dma((3,)), dma((each,)), dma((each,)), dma((4,)),
            dma((8,)), dma((8,)), dma((each,)), dma((each,)),
            dma((2,)), dma((2,)), dma((2,)), dma((2,)),
        ],
        compiler_params=pltpu.CompilerParams(collective_id=0, has_side_effects=True, vmem_limit_bytes=63 << 20),
    )(staves, weights, replica, start.T, length.T, first, twiddle, second, smooth)
    return out[0].T, out[1].T


def solution(mesh):
    in_specs = (
        P(None, "ping", "band", None, None),
        P(None, "band", None, None),
        P(),
        P("ping", "band"),
        P("ping", "band"),
    )
    out_specs = (P("ping", "band"), P("ping", "band"))
    step = functools.partial(local, mesh.shape["band"], mesh.shape["ping"])
    return jax.shard_map(step, mesh=mesh, in_specs=in_specs, out_specs=out_specs, check_vma=False)
```

time: 48.9 us -> 45.7 us (0.935)
  Pallas kernels: 45.6 us -> 43.6 us
  local copies, waits for them, and re-layouts: 2.53 us -> 1.28 us
    unnamed x2 -> x0, local copies, waits for them, and re-layouts: 2.53 us -> none
    pallas_call x1, Pallas kernels: 45.6 us -> 43.6 us  [local(): pl.pallas_call(functools.partial(kernel, bands, blocks), out_shape=jax.Sh...]
    transpose x0 -> x1, local copies, waits for them, and re-layouts: none -> 1.28 us  [local(): return (out[0].T, out[1].T)]
where the time goes in v3:
time: 45.7 us; the launch traced here: 45.6 us
  Pallas kernels  43.6 us (95%)
  local copies, waits for them, and re-layouts  1.28 us (3%)
  between operations  0.64 us (1%)
    pallas_call x1, Pallas kernels, local(): pl.pallas_call(functools.partial(kernel, bands, blocks), out_shape=jax.Sh...  43.6 us
    transpose x1, local copies, waits for them, and re-layouts, local(): return (out[0].T, out[1].T)  1.28 us

profile of v3, /device:TPU:1, one launch (start us, length us, event | category | flops | bytes accessed | tf_op | source)
XLA Modules:
  0.0 45.6 jit_solution(10901179171934830172)
XLA Ops:
  0.6 43.6 %shard_map.104 = f32[2,8,16]{2,1,0:T(8,128)} custom-call(bf16[2,16,4,8,512]{4,3,2,1,0:T(8,128)(2,1)} %staves.1, bf16[2,4,512,512]{3,2,1,0:T(8,128)(2,1)} %weights.1, f32[2,2048]{1,0:T(2,128)} %replica.1, s32[8,16]{1,0:T(8,128)} %bitcast.10, s32[8,16]{1,0:T(8,128)} %bitcast.11, bf16[512,512]{1,0:T(8,128)(2,1)} %constant.8.clone.first_in, ...), custom_call_target="tpu_custom_call" | custom-call | tf_op jit(solution)/shard_map/pallas_call | solution.py:336
  44.3 1.3 %slice_bitcast_fusion = (f32[16,8]{0,1:T(8,128)}, f32[16,8]{0,1:T(8,128)}) fusion(f32[2,8,16]{2,1,0:T(8,128)} %shard_map.104), kind=kLoop, calls=%fused_computation | loop fusion | bytes 2048 | tf_op jit(solution)/shard_map/transpose | solution.py:369

commit v4 on v3

--- a/solution.py
+++ b/solution.py
@@ -21,11 +21,18 @@
     total = SPLIT * BINS
     turn = 2.0 * math.pi / total
     t1 = np.arange(SPLIT)
-    half_of, plane = np.divmod(np.arange(sources), sources // 2)
-    source = (plane // ROW * 2 + half_of) * ROW + plane % ROW
-    band = (source[None, :] * bands_each + np.arange(bands_each)[:, None]).reshape(-1)
-    angle = ((t1[:, None] * band[None, :] * BINS) % total) * turn
-    first = np.block([[np.cos(angle), -np.sin(angle)], [np.sin(angle), np.cos(angle)]])
+    place = np.arange(sources // 2)
+    first = []
+    for z in range(2):
+        source = (place // ROW * 2 + z) * ROW + place % ROW
+        columns = []
+        for pair in range(bands_each // 2):
+            band = (source[None, :] * bands_each + pair * 2 + np.arange(2)[:, None]).reshape(-1)
+            angle = ((t1[:, None] * band[None, :] * BINS) % total) * turn
+            cos, sin = np.cos(angle), np.sin(angle)
+            columns.append(np.block([[cos, -sin], [sin, cos]]))
+        first.append(np.concatenate(columns, axis=1))
+    first = np.stack(first)
     lane = np.arange(128)
     ping, small = lane // BINS, lane % BINS
     angle = ((t1[:, None] * small[None, :]) % total) * turn
@@ -47,7 +54,7 @@
     bands, blocks,
     staves, weights, replica, start, length, first_in, twiddle_in, second_in, smooth_in,
     result,
-    qbuf, tbuf, rep, win, xbuf, wbuf, sbuf, over, gathered, plane, beyond, fbuf, rhs, ebuf,
+    qbuf, tbuf, rep, win, xbuf, wbuf, sbuf, over, gathered, plane, beyond, fbuf, rhs, sums, ebuf,
     first, twiddle, second, smooth, near, acc, hrecv,
     qsem, xsem, wsem, csem, psend, precv, zsend, zrecv, nsem, msem, hsem, gsem,
 ):
@@ -236,8 +243,8 @@
 
     half = columns * ROW * 16
 
-    def unpack(n, z, tiles):
-        fbuf[n, pl.ds(z * half, half)] = tiles.astype(jnp.float32).reshape(half, 128)
+    def unpack(n, slot, tiles):
+        fbuf[n, slot] = tiles.astype(jnp.float32).reshape(half, 128)
 
     for copy in consts:
         copy.wait()
@@ -249,9 +256,9 @@
 
     for k in range(2):
         scattered(sbuf.at[k, here_z], plane.at[k], k).wait_recv()
-        unpack(k, here_z, plane[k])
+        unpack(k, 0, plane[k])
         scattered(over.at[k], beyond.at[k], 6 + k).wait_recv()
-        unpack(k, there_z, beyond[k])
+        unpack(k, 1, beyond[k])
 
     def window(b, g):
         sm = jnp.dot(ebuf[b], smooth[:, g * 128 : (g + 1) * 128], preferred_element_type=jnp.float32)
@@ -263,15 +270,28 @@
         acc[g, pl.ds(b, 1), :] = e
         acc[g, pl.ds(b + 8, 1), :] = m
 
-    def transform(half_of, pair):
+    def gather(half_of, pair, slot, late):
+        base = (slot * 2 + late) * 2 * 2 * size
         for i in range(2):
-            for j in range(4):
+            for j in range(2):
                 for h in range(2):
                     q = pair * 2 + h
-                    n, at_row = (j, half_of * 4 + q) if j < 2 else (2 + half_of, (j - 2) * 4 + q)
-                    part = fbuf[n, pl.ds(i * 8 + at_row, bands, stride=16), :]
-                    rhs[pl.ds((i * each + j) * bands, bands), h * 128 : (h + 1) * 128] = part.astype(jnp.bfloat16)
-        out = jnp.dot(first[...], rhs[...], preferred_element_type=jnp.float32)
+                    n, at_row = (2 + half_of, j * 4 + q) if late else (j, half_of * 4 + q)
+                    part = fbuf[n, slot, pl.ds(i * 8 + at_row, size, stride=16), :]
+                    rhs[pair, pl.ds(base + (i * 2 + j) * size, size), h * 128 : (h + 1) * 128] = part.astype(jnp.bfloat16)
+
+    def prepare(half_of, pair):
+        for slot, late in ((0, 0), (0, 1), (1, 0)):
+            gather(half_of, pair, slot, late)
+        span = 8 * size
+        sums[pair] = jnp.dot(first[here_z], rhs[pair, :span], preferred_element_type=jnp.float32) + jnp.dot(
+            first[there_z, :, : span // 2], rhs[pair, span : span * 3 // 2], preferred_element_type=jnp.float32)
+
+    def transform(half_of, pair):
+        gather(half_of, pair, 1, 1)
+        span = 8 * size
+        out = sums[pair] + jnp.dot(
+            first[there_z, :, span // 2 :], rhs[pair, span * 3 // 2 :], preferred_element_type=jnp.float32)
         for h in range(2):
             re, im = out[:SPLIT, h * 128 : (h + 1) * 128], out[SPLIT:, h * 128 : (h + 1) * 128]
             c, s = twiddle[0], twiddle[1]
@@ -284,19 +304,18 @@
     partial = beside(acc.at[1], hrecv, hsem, gsem)
     for h in range(2):
         scattered(sbuf.at[2 + h, here_z], plane.at[2 + h], 2 + h).wait_recv()
-        unpack(2 + h, here_z, plane[2 + h])
+        unpack(2 + h, 0, plane[2 + h])
+        for pair in range(2):
+            prepare(h, pair)
         across(gathered.at[h], beyond.at[2 + h], 2 + h).wait_recv()
-        unpack(2 + h, there_z, beyond[2 + h])
-
-        @pl.loop(0, 2)
-        def _(pair):
+        unpack(2 + h, 1, beyond[2 + h])
+        for pair in range(2):
             transform(h, pair)
 
         if h == 1:
             send(partial)
 
-        @pl.loop(0, 4)
-        def _(q):
+        for q in range(4):
             window(h * 4 + q, 0)
 
     receive(partial)
@@ -350,8 +369,9 @@
             pltpu.VMEM((2, *plane), bf16),
             pltpu.VMEM((each, *plane), bf16),
             pltpu.VMEM((each, *plane), bf16),
-            pltpu.VMEM((each, bands * 16, 128), f32),
-            pltpu.VMEM((2 * each * bands, 256), bf16),
+            pltpu.VMEM((each, 2, bands * 8, 128), f32),
+            pltpu.VMEM((2, 2 * each * bands, 256), bf16),
+            pltpu.VMEM((2, 2 * SPLIT, 256), f32),
             pltpu.VMEM((8, SPLIT, 128), bf16),
             pltpu.VMEM(first.shape, bf16),
             pltpu.VMEM(twiddle.shape, f32),

time: 45.7 us -> 44.7 us (0.978)
  Pallas kernels: 43.6 us -> 42.6 us
    pallas_call x1, Pallas kernels: 43.6 us -> 42.6 us  [local(): pl.pallas_call(functools.partial(kernel, bands, blocks), out_shape=jax.Sh...]
where the time goes in v4:
time: 44.7 us; the launch traced here: 44.5 us
  Pallas kernels  42.6 us (95%)
  local copies, waits for them, and re-layouts  1.28 us (3%)
  between operations  0.64 us (1%)
    pallas_call x1, Pallas kernels, local(): pl.pallas_call(functools.partial(kernel, bands, blocks), out_shape=jax.Sh...  42.6 us
    transpose x1, local copies, waits for them, and re-layouts, local(): return (out[0].T, out[1].T)  1.28 us

profile of v4, /device:TPU:1, one launch (start us, length us, event | category | flops | bytes accessed | tf_op | source)
XLA Modules:
  0.0 44.5 jit_solution(3848718480323537327)
XLA Ops:
  0.6 42.6 %shard_map.104 = f32[2,8,16]{2,1,0:T(8,128)} custom-call(bf16[2,16,4,8,512]{4,3,2,1,0:T(8,128)(2,1)} %staves.1, bf16[2,4,512,512]{3,2,1,0:T(8,128)(2,1)} %weights.1, f32[2,2048]{1,0:T(2,128)} %replica.1, s32[8,16]{1,0:T(8,128)} %bitcast.10, s32[8,16]{1,0:T(8,128)} %bitcast.11, bf16[2,512,256]{2,1,0:T(8,128)(2,1)} %constant.8.clone.first_in, ...), custom_call_target="tpu_custom_call" | custom-call | tf_op jit(solution)/shard_map/pallas_call | solution.py:355
  43.3 1.3 %slice_bitcast_fusion = (f32[16,8]{0,1:T(8,128)}, f32[16,8]{0,1:T(8,128)}) fusion(f32[2,8,16]{2,1,0:T(8,128)} %shard_map.104), kind=kLoop, calls=%fused_computation | loop fusion | bytes 2048 | tf_op jit(solution)/shard_map/transpose | solution.py:389

commit v5 on v4

--- a/solution.py
+++ b/solution.py
@@ -56,7 +56,7 @@
     result,
     qbuf, tbuf, rep, win, xbuf, wbuf, sbuf, over, gathered, plane, beyond, fbuf, rhs, sums, ebuf,
     first, twiddle, second, smooth, near, acc, hrecv,
-    qsem, xsem, wsem, csem, psend, precv, zsend, zrecv, nsem, msem, hsem, gsem,
+    qsem, xsem, wsem, csem, psend, precv, zsend, zrecv, nsem, msem, hsem, gsem, met,
 ):
     me, block = lax.axis_index("band"), lax.axis_index("ping")
     each = wbuf.shape[0]
@@ -75,11 +75,12 @@
     barrier = pltpu.get_barrier_semaphore()
     pl.semaphore_signal(barrier, inc=1, device_id=at(y, there_z, r), device_id_type=MESH)
 
-    @pl.loop(1, columns * ROW)
-    def _(i):
-        place = lax.rem(mine + i, columns * ROW)
-        pl.semaphore_signal(
-            barrier, inc=1, device_id=at(lax.div(place, ROW), here_z, lax.rem(place, ROW)), device_id_type=MESH)
+    def along(step):
+        place = lax.rem(mine + step + columns * ROW, columns * ROW)
+        return at(lax.div(place, ROW), here_z, lax.rem(place, ROW))
+
+    for step in (1, -1, 2, -2):
+        pl.semaphore_signal(barrier, inc=1, device_id=along(step), device_id_type=MESH)
 
     @pl.when(block > 0)
     def _():
@@ -189,6 +190,15 @@
     win[0:8] = low
     win[8:16] = low + times[8:]
 
+    def tell(turn):
+        for side in range(2):
+            pl.semaphore_signal(
+                met.at[turn, side], inc=1, device_id=along((2 << turn) * (1 - 2 * side)), device_id_type=MESH)
+
+    def hear(turn):
+        for side in range(2):
+            pl.semaphore_wait(met.at[turn, side], 1)
+
     def beams(k, c):
         x = xbuf[k].astype(jnp.float32).reshape(2 * 128, -1).astype(jnp.bfloat16)
         r0, r1 = rep[k, 0:1, :], rep[k, 1:2, :]
@@ -213,9 +223,14 @@
             put(k, c, beams(k, c))
 
     early(0)
-    pl.semaphore_wait(barrier, size + sides)
+    pl.semaphore_wait(barrier, 5 + sides)
+    tell(0)
     across(sbuf.at[0, there_z], over.at[0], 0).start()
     send(edges)
+    early(1)
+    across(sbuf.at[1, there_z], over.at[1], 1).start()
+    hear(0)
+    tell(1)
     for k in (2, 3):
         for copy in loads[k]:
             copy.wait()
@@ -224,11 +239,11 @@
         for h in range(2):
             part = slice(4 * h, 4 * h + 4)
             put(2 + h, c, [a[0][:, part], b[0][:, part], a[1][:, part], b[1][:, part]])
+        hear(1 + c)
+        if c == 0:
+            tell(2)
     for h in range(2):
         scatter(sbuf.at[2 + h, there_z], gathered.at[h], 4 + h)
-    early(1)
-    across(sbuf.at[1, there_z], over.at[1], 1).start()
-
     scattered(sbuf.at[2, there_z], gathered.at[0], 4).wait_recv()
     across(gathered.at[0], beyond.at[2], 2).start()
     for n in range(3):
@@ -383,6 +398,7 @@
             dma((3,)), dma((each,)), dma((each,)), dma((4,)),
             dma((8,)), dma((8,)), dma((each,)), dma((each,)),
             dma((2,)), dma((2,)), dma((2,)), dma((2,)),
+            pltpu.SemaphoreType.REGULAR((3, 2)),
         ],
         compiler_params=pltpu.CompilerParams(collective_id=0, has_side_effects=True, vmem_limit_bytes=63 << 20),
     )(staves, weights, replica, start.T, length.T, first, twiddle, second, smooth)

time: 44.7 us -> 43.1 us (0.964)
  Pallas kernels: 42.6 us -> 40.6 us
    pallas_call x1, Pallas kernels: 42.6 us -> 40.6 us  [local(): pl.pallas_call(functools.partial(kernel, bands, blocks), out_shape=jax.Sh...]
where the time goes in v5:
time: 43.1 us; the launch traced here: 42.6 us
  Pallas kernels  40.6 us (94%)
  local copies, waits for them, and re-layouts  1.28 us (3%)
  between operations  0.64 us (1%)
    pallas_call x1, Pallas kernels, local(): pl.pallas_call(functools.partial(kernel, bands, blocks), out_shape=jax.Sh...  40.6 us
    transpose x1, local copies, waits for them, and re-layouts, local(): return (out[0].T, out[1].T)  1.28 us

profile of v5, /device:TPU:1, one launch (start us, length us, event | category | flops | bytes accessed | tf_op | source)
XLA Modules:
  0.0 42.6 jit_solution(11989369872583792343)
XLA Ops:
  0.6 40.6 %shard_map.104 = f32[2,8,16]{2,1,0:T(8,128)} custom-call(bf16[2,16,4,8,512]{4,3,2,1,0:T(8,128)(2,1)} %staves.1, bf16[2,4,512,512]{3,2,1,0:T(8,128)(2,1)} %weights.1, f32[2,2048]{1,0:T(2,128)} %replica.1, s32[8,16]{1,0:T(8,128)} %bitcast.10, s32[8,16]{1,0:T(8,128)} %bitcast.11, bf16[2,512,256]{2,1,0:T(8,128)(2,1)} %constant.8.clone.first_in, ...), custom_call_target="tpu_custom_call" | custom-call | tf_op jit(solution)/shard_map/pallas_call | solution.py:370
  41.3 1.3 %slice_bitcast_fusion = (f32[16,8]{0,1:T(8,128)}, f32[16,8]{0,1:T(8,128)}) fusion(f32[2,8,16]{2,1,0:T(8,128)} %shard_map.104), kind=kLoop, calls=%fused_computation | loop fusion | bytes 2048 | tf_op jit(solution)/shard_map/transpose | solution.py:405

commit v6 on v5

--- a/solution.py
+++ b/solution.py
@@ -79,7 +79,7 @@
         place = lax.rem(mine + step + columns * ROW, columns * ROW)
         return at(lax.div(place, ROW), here_z, lax.rem(place, ROW))
 
-    for step in (1, -1, 2, -2):
+    for step in (1, -1, 2, -2, 3, -3, 4, -4):
         pl.semaphore_signal(barrier, inc=1, device_id=along(step), device_id_type=MESH)
 
     @pl.when(block > 0)
@@ -193,7 +193,7 @@
     def tell(turn):
         for side in range(2):
             pl.semaphore_signal(
-                met.at[turn, side], inc=1, device_id=along((2 << turn) * (1 - 2 * side)), device_id_type=MESH)
+                met.at[turn, side], inc=1, device_id=along((4 << turn) * (1 - 2 * side)), device_id_type=MESH)
 
     def hear(turn):
         for side in range(2):
@@ -223,7 +223,7 @@
             put(k, c, beams(k, c))
 
     early(0)
-    pl.semaphore_wait(barrier, 5 + sides)
+    pl.semaphore_wait(barrier, 9 + sides)
     tell(0)
     across(sbuf.at[0, there_z], over.at[0], 0).start()
     send(edges)
@@ -239,9 +239,7 @@
         for h in range(2):
             part = slice(4 * h, 4 * h + 4)
             put(2 + h, c, [a[0][:, part], b[0][:, part], a[1][:, part], b[1][:, part]])
-        hear(1 + c)
-        if c == 0:
-            tell(2)
+    hear(1)
     for h in range(2):
         scatter(sbuf.at[2 + h, there_z], gathered.at[h], 4 + h)
     scattered(sbuf.at[2, there_z], gathered.at[0], 4).wait_recv()
@@ -398,7 +396,7 @@
             dma((3,)), dma((each,)), dma((each,)), dma((4,)),
             dma((8,)), dma((8,)), dma((each,)), dma((each,)),
             dma((2,)), dma((2,)), dma((2,)), dma((2,)),
-            pltpu.SemaphoreType.REGULAR((3, 2)),
+            pltpu.SemaphoreType.REGULAR((2, 2)),
         ],
         compiler_params=pltpu.CompilerParams(collective_id=0, has_side_effects=True, vmem_limit_bytes=63 << 20),
     )(staves, weights, replica, start.T, length.T, first, twiddle, second, smooth)

time: 43.1 us -> 42.9 us (level)
  no operation moved by 1% of the time
where the time goes in v6:
time: 42.9 us; the launch traced here: 42.8 us
  Pallas kernels  40.9 us (95%)
  local copies, waits for them, and re-layouts  1.28 us (3%)
  between operations  0.64 us (1%)
    pallas_call x1, Pallas kernels, local(): pl.pallas_call(functools.partial(kernel, bands, blocks), out_shape=jax.Sh...  40.9 us
    transpose x1, local copies, waits for them, and re-layouts, local(): return (out[0].T, out[1].T)  1.28 us

profile of v6, /device:TPU:1, one launch (start us, length us, event | category | flops | bytes accessed | tf_op | source)
XLA Modules:
  0.0 42.8 jit_solution(111430805394304171)
XLA Ops:
  0.6 40.9 %shard_map.104 = f32[2,8,16]{2,1,0:T(8,128)} custom-call(bf16[2,16,4,8,512]{4,3,2,1,0:T(8,128)(2,1)} %staves.1, bf16[2,4,512,512]{3,2,1,0:T(8,128)(2,1)} %weights.1, f32[2,2048]{1,0:T(2,128)} %replica.1, s32[8,16]{1,0:T(8,128)} %bitcast.10, s32[8,16]{1,0:T(8,128)} %bitcast.11, bf16[2,512,256]{2,1,0:T(8,128)(2,1)} %constant.8.clone.first_in, ...), custom_call_target="tpu_custom_call" | custom-call | tf_op jit(solution)/shard_map/pallas_call | solution.py:368
  41.5 1.3 %slice_bitcast_fusion = (f32[16,8]{0,1:T(8,128)}, f32[16,8]{0,1:T(8,128)}) fusion(f32[2,8,16]{2,1,0:T(8,128)} %shard_map.104), kind=kLoop, calls=%fused_computation | loop fusion | bytes 2048 | tf_op jit(solution)/shard_map/transpose | solution.py:403

commit v7 on v6

--- a/solution.py
+++ b/solution.py
@@ -199,8 +199,10 @@
         for side in range(2):
             pl.semaphore_wait(met.at[turn, side], 1)
 
-    def beams(k, c):
-        x = xbuf[k].astype(jnp.float32).reshape(2 * 128, -1).astype(jnp.bfloat16)
+    def rows_of(k):
+        return xbuf[k].astype(jnp.float32).reshape(2 * 128, -1).astype(jnp.bfloat16)
+
+    def beams(k, c, x):
         r0, r1 = rep[k, 0:1, :], rep[k, 1:2, :]
         here = pl.ds(c * 256, 256)
         p0 = jnp.dot(x, wbuf[k, 0, :, here], preferred_element_type=jnp.float32)
@@ -219,8 +221,9 @@
     def early(k):
         for copy in loads[k]:
             copy.wait()
+        x = rows_of(k)
         for c in range(chunks):
-            put(k, c, beams(k, c))
+            put(k, c, beams(k, c, x))
 
     early(0)
     pl.semaphore_wait(barrier, 9 + sides)
@@ -234,8 +237,9 @@
     for k in (2, 3):
         for copy in loads[k]:
             copy.wait()
+    x2, x3 = rows_of(2), rows_of(3)
     for c in range(chunks):
-        a, b = beams(2, c), beams(3, c)
+        a, b = beams(2, c, x2), beams(3, c, x3)
         for h in range(2):
             part = slice(4 * h, 4 * h + 4)
             put(2 + h, c, [a[0][:, part], b[0][:, part], a[1][:, part], b[1][:, part]])

time: 42.9 us -> 42.9 us (level)
  no operation moved by 1% of the time
where the time goes in v7:
time: 42.9 us; the launch traced here: 42.8 us
  Pallas kernels  40.9 us (95%)
  local copies, waits for them, and re-layouts  1.28 us (3%)
  between operations  0.64 us (1%)
    pallas_call x1, Pallas kernels, local(): pl.pallas_call(functools.partial(kernel, bands, blocks), out_shape=jax.Sh...  40.9 us
    transpose x1, local copies, waits for them, and re-layouts, local(): return (out[0].T, out[1].T)  1.28 us

profile of v7, /device:TPU:1, one launch (start us, length us, event | category | flops | bytes accessed | tf_op | source)
XLA Modules:
  0.0 42.8 jit_solution(13928381916998604800)
XLA Ops:
  0.6 40.9 %shard_map.104 = f32[2,8,16]{2,1,0:T(8,128)} custom-call(bf16[2,16,4,8,512]{4,3,2,1,0:T(8,128)(2,1)} %staves.1, bf16[2,4,512,512]{3,2,1,0:T(8,128)(2,1)} %weights.1, f32[2,2048]{1,0:T(2,128)} %replica.1, s32[8,16]{1,0:T(8,128)} %bitcast.10, s32[8,16]{1,0:T(8,128)} %bitcast.11, bf16[2,512,256]{2,1,0:T(8,128)(2,1)} %constant.8.clone.first_in, ...), custom_call_target="tpu_custom_call" | custom-call | tf_op jit(solution)/shard_map/pallas_call | solution.py:372
  41.5 1.3 %slice_bitcast_fusion = (f32[16,8]{0,1:T(8,128)}, f32[16,8]{0,1:T(8,128)}) fusion(f32[2,8,16]{2,1,0:T(8,128)} %shard_map.104), kind=kLoop, calls=%fused_computation | loop fusion | bytes 2048 | tf_op jit(solution)/shard_map/transpose | solution.py:407
